TPU v7x, 128 devices: a whole 4x4x4 slice. The times are simulated.
128 devices in a mesh: row: 32 (over z_lo, y, x), col: 4 (over z_hi, core).
Axes of the slice: x: 4, y: 4, z: 4 (z_hi: 2, z_lo: 2; z = z_hi * 2 + z_lo), core: 2. Of those that a mesh axis runs over, the one named last changes fastest.
Arguments:
- panel_tiles: float32 [65536, 1024], P('row', 'col'), may hold values from -48 to 48
- left_u: bfloat16 [65536, 6144], P('row', 'col'), may hold values from -8 to 8
- earlier_right_factors: bfloat16 [65536, 6144], P('row', 'col'), may hold values from -0.25 to 0.25
- tile_global_index: int32 [64], replicated, may hold values from 0 to 63, as said below
Outputs:
- panel_factor: float32 [65536, 1024], P('row', 'col')
Inputs may be any that keep to these rules, and one draw needn't show every extreme that they name: `tile_global_index`: A permutation; slot pivot, the one numbered 0, holds the diagonal tile.
All inputs are finite; a program needn't handle non-finite values.
Results may differ from a plain program's by a relative error of at most 0.00053.
Values may be sent and summed in bfloat16 or wider, within the bound.
No kernel may reach another device: no remote copies, remote signals or barrier semaphores. Data moves between devices by JAX's collectives and lax.ppermute only.
A program may use at most 128 MiB of HBM per device.

v0:
```python
import jax
import jax.numpy as jnp
from jax import lax
from jax.sharding import Mesh
from jax.sharding import PartitionSpec as P

TILE = 1024
RANK = 256
TILE_DEV = 2
COL_DEV = 6
ROW = ("row_0", "row_1", "row_2")


def from_root(value, axis, source):
    kept = jnp.where(lax.axis_index(axis) == source, value, 0).astype(value.dtype)
    return lax.psum(kept, axis)


def split_up(value, dim, devices):
    shape = value.shape
    parts = value.reshape(*shape[:dim], devices, shape[dim] // devices, *shape[dim + 1 :])
    return jnp.moveaxis(parts, dim, 0)


def summed_on_arrival(value, axis, dim):
    devices = lax.axis_size(axis)
    parts = lax.all_to_all(split_up(value, dim, devices), axis, 0, 0, tiled=True)
    return jnp.sum(parts, axis=0)


def broadcast_by_axis(value, axes, root):
    value = jnp.where(lax.axis_index(axes) == root, value, jnp.zeros_like(value))
    for axis in axes:
        value = lax.psum(value, axis)
    return value


def local(panel_tiles, left_u, earlier_right_factors, tile_global_index):
    tile_count = tile_global_index.shape[0]
    pivot_position = jnp.sum(
        jnp.where(tile_global_index == 0, jnp.arange(tile_count, dtype=jnp.int32), 0)
    )
    owner_row = pivot_position // TILE_DEV
    local_slot = pivot_position % TILE_DEV
    my_row = lax.axis_index(ROW)
    my_col = lax.axis_index("col")
    col_width = panel_tiles.shape[1]
    pivot_left = lax.dynamic_slice_in_dim(left_u, local_slot * TILE, TILE, 0)
    pivot_right = lax.dynamic_slice_in_dim(earlier_right_factors, local_slot * TILE, TILE, 0)
    pivot_left, pivot_right = (
        from_root(pivot_left, ROW, owner_row),
        from_root(pivot_right, ROW, owner_row),
    )
    left_blocks = left_u.reshape(TILE_DEV, TILE, COL_DEV, RANK)
    right_blocks = earlier_right_factors.reshape(TILE_DEV, TILE, COL_DEV, RANK)
    pivot_triple = pivot_right.reshape(TILE, COL_DEV, RANK)
    inner_small = jnp.einsum(
        "tbjr,bjs->tjrs", right_blocks, pivot_triple, preferred_element_type=jnp.float32
    ).astype(jnp.bfloat16)
    left_small = jnp.einsum(
        "tbjr,tjrs->tbjs", left_blocks, inner_small, preferred_element_type=jnp.float32
    ).astype(jnp.bfloat16)
    update_terms = jnp.einsum(
        "nk,mk->nm",
        left_small.reshape(TILE_DEV * TILE, COL_DEV * RANK),
        pivot_left,
        preferred_element_type=jnp.float32,
    )
    own_sums = summed_on_arrival(update_terms, "col", 1)
    updated_tiles = lax.all_gather(panel_tiles - own_sums, "col", axis=1, tiled=True)
    diagonal = lax.dynamic_slice_in_dim(updated_tiles, local_slot * TILE, TILE, 0)
    identity = jnp.eye(TILE, dtype=jnp.float32)
    cholesky_factor = jnp.linalg.cholesky(diagonal)
    inverted_factor = lax.linalg.triangular_solve(
        cholesky_factor, identity, left_side=True, lower=True
    )
    rows_inv = lax.dynamic_slice_in_dim(inverted_factor, my_col * col_width, col_width, 0)
    rows_inv = broadcast_by_axis(rows_inv, ROW, owner_row)
    solved_rows = lax.dot_general(
        updated_tiles,
        rows_inv,
        (((1,), (1,)), ((), ())),
        precision=lax.Precision.HIGHEST,
        preferred_element_type=jnp.float32,
    )
    factor_cols = lax.dynamic_slice_in_dim(cholesky_factor, my_col * col_width, col_width, 1)
    row_tiles = jnp.arange(TILE_DEV * TILE, dtype=jnp.int32) // TILE
    chosen_rows = jnp.logical_and(my_row == owner_row, row_tiles == local_slot)
    return jnp.where(chosen_rows[:, None], jnp.tile(factor_cols, (TILE_DEV, 1)), solved_rows)


def solution(mesh):
    split = Mesh(
        mesh.devices.reshape(2, 4, 4, mesh.shape["col"]), ("row_0", "row_1", "row_2", "col")
    )
    return jax.shard_map(
        local,
        mesh=split,
        in_specs=(P(ROW, "col"), P(ROW, "col"), P(ROW, "col"), P()),
        out_specs=P(ROW, "col"),
        check_vma=False,
    )
```

profile of v0, /device:TPU:0, one launch (start us, length us, event | category | flops | bytes accessed | tf_op | source)
XLA Modules:
  0.0 1110.6 jit_solution(5675291476867327517)
XLA Ops:
  10.4 5.9 constant_dynamic-slice_fusion.3
  30.5 13.3 %reshape.130 = bf16[2,1024,6,256]{3,2,1,0:T(8,128)(2,1)} reshape(bf16[2048,1536]{1,0:T(8,128)(2,1)} %param.5) | data formatting | bytes 12582912 | tf_op jit(solution)/shard_map/reshape | solution.py:54
  43.8 13.4 %reshape.129 = bf16[2,1024,6,256]{3,2,1,0:T(8,128)(2,1)} reshape(bf16[2048,1536]{1,0:T(8,128)(2,1)} %param.6) | data formatting | bytes 12582912 | tf_op jit(solution)/shard_map/reshape | solution.py:55
  57.2 310.4 %all-reduce.13.cloned.1.call-done = (bf16[1024,6,256]{0,2,1:T(8,128)(2,1)}, bf16[4,256,1536]{2,1,0:T(8,128)(2,1)}) async-done(((bf16[1024,6,256]{0,2,1:T(8,128)(2,1)}, bf16[4,256,1536]{2,1,0:T(8,128)(2,1)}), (bf16[1024,6,256]{0,2,1:T(8,128)(2,1)}, bf16[4,256,1536]{2,1,0:T(8,128)(2,1)})) %all-reduce.13.cloned.1.call-update) | async-done | bytes 6291472 | tf_op jit(solution)/shard_map/psum | solution.py:16
  367.6 16.6 %convert_bitcast_fusion = bf16[2,1024,6,256]{1,3,2,0:T(8,128)(2,1)} fusion(bf16[2,1024,6,256]{3,2,1,0:T(8,128)(2,1)} %reshape.130, bf16[2,1024,6,256]{3,2,1,0:T(8,128)(2,1)} %reshape.129, bf16[1024,6,256]{0,2,1:T(8,128)(2,1)} %get-tuple-element.21), kind=kOutput, calls=%fused_computation.6 | convolution fusion | flops 3225157632 | bytes 22020096 | tf_op jit(solution)/shard_map/tbjr,tjrs->tbjs/dot_general | solution.py:60
  384.2 12.7 %copy.23 = bf16[2,1024,6,256]{1,0,3,2:T(2,128)(2,1)} copy(bf16[2,1024,6,256]{1,3,2,0:T(8,128)(2,1)} %convert_bitcast_fusion) | data formatting | bytes 12582912 | tf_op jit(solution)/shard_map/convert_element_type | solution.py:62
  396.8 11.3 %reshape.133 = bf16[2048,1536,1]{0,1,2:T(8,128)(2,1)} reshape(bf16[2,1024,6,256]{1,0,3,2:T(2,128)(2,1)} %copy.23) | data formatting | bytes 12582912 | tf_op jit(solution)/shard_map/reshape | solution.py:65
  408.2 11.0 convolution_bitcast_fusion
  426.8 92.7 %all-to-all-done = f32[4,2048,256]{2,1,0:T(8,128)} async-done(((f32[4,2048,256]{2,1,0:T(8,128)}), f32[4,2048,256]{2,1,0:T(8,128)}, u32[]{:S(2)}, u32[]{:S(2)}) %all-to-all-start) | async-done | bytes 8388640 | tf_op jit(solution)/shard_map/all_to_all | solution.py:27
  534.0 58.3 %all-gather.2.cloned.1.call-done = f32[2048,1024]{0,1:T(8,128)} async-done(((f32[2048,256]{0,1:T(8,128)}), f32[2048,1024]{0,1:T(8,128)}) %all-gather.2.cloned.1.call-update) | async-done | bytes 8388624 | tf_op jit(solution)/shard_map/all_gather | solution.py:70
  597.1 5.7 copy.29
  609.3 11.7 %cholesky.223 = f32[128,128]{1,0:T(8,128)S(1)} custom-call(f32[128,128]{1,0:T(8,128)S(1)} %cholesky.580), custom_call_target="Cholesky" | custom-call | tf_op jit(solution)/shard_map/jit(cholesky)/cholesky | solution.py:73
  623.5 9.8 custom-call.62
  637.3 11.9 %cholesky.244 = f32[128,128]{1,0:T(8,128)S(1)} custom-call(f32[128,128]{1,0:T(8,128)S(1)} %cholesky.584), custom_call_target="Cholesky" | custom-call | tf_op jit(solution)/shard_map/jit(cholesky)/cholesky | solution.py:73
  649.8 9.8 custom-call.63
  662.9 11.7 %cholesky.468 = f32[128,128]{1,0:T(8,128)S(1)} custom-call(f32[128,128]{1,0:T(8,128)S(1)} %cholesky.589), custom_call_target="Cholesky" | custom-call | tf_op jit(solution)/shard_map/jit(cholesky)/cholesky | solution.py:73
  675.3 9.8 custom-call.64
  688.6 11.9 %cholesky.487 = f32[128,128]{1,0:T(8,128)S(1)} custom-call(f32[128,128]{1,0:T(8,128)S(1)} %cholesky.594), custom_call_target="Cholesky" | custom-call | tf_op jit(solution)/shard_map/jit(cholesky)/cholesky | solution.py:73
  701.2 9.8 custom-call.65
  714.5 11.7 %cholesky.506 = f32[128,128]{1,0:T(8,128)S(1)} custom-call(f32[128,128]{1,0:T(8,128)S(1)} %cholesky.599), custom_call_target="Cholesky" | custom-call | tf_op jit(solution)/shard_map/jit(cholesky)/cholesky | solution.py:73
  726.8 10.2 custom-call.66
  740.3 11.7 %cholesky.526 = f32[128,128]{1,0:T(8,128)S(1)} custom-call(f32[128,128]{1,0:T(8,128)S(1)} %cholesky.604), custom_call_target="Cholesky" | custom-call | tf_op jit(solution)/shard_map/jit(cholesky)/cholesky | solution.py:73
  752.7 9.8 custom-call.67
  765.5 11.7 %cholesky.546 = f32[128,128]{1,0:T(8,128)S(1)} custom-call(f32[128,128]{1,0:T(8,128)S(1)} %cholesky.609), custom_call_target="Cholesky" | custom-call | tf_op jit(solution)/shard_map/jit(cholesky)/cholesky | solution.py:73
  777.8 9.8 custom-call.68
  790.3 11.7 %cholesky.564 = f32[128,128]{1,0:T(8,128)S(1)} custom-call(f32[128,128]{1,0:T(8,128)S(1)} %convolution_subtract_fusion.11), custom_call_target="Cholesky" | custom-call | tf_op jit(solution)/shard_map/jit(cholesky)/cholesky | solution.py:73
  817.1 23.1 %while.1 = (s32[]{:T(128)}, f32[1024,1024]{1,0:T(8,128)}, s32[8,2]{0,1:T(2,128)S(1)}, f32[8,128,128]{2,1,0:T(8,128)S(1)}, s32[]{:T(128)}) while((s32[]{:T(128)}, f32[1024,1024]{1,0:T(8,128)}, s32[8,2]{0,1:T(2,128)S(1)}, f32[8,128,128]{2,1,0:T(8,128)S(1)}, s32[]{:T(128)}) %tuple.58), condition=%wide.while_cond, body=%wide.while_body.sunk | while | flops 2 | bytes 131189 | solution.py:74
  840.2 78.8 %custom-call.69 = f32[8,128,128]{1,2,0:T(8,128)S(1)} custom-call(f32[8,128,128]{2,1,0:T(8,128)S(1)} %get-tuple-element.12), custom_call_target="InvertDiagBlocksLowerTriangular" | custom-call | tf_op jit(solution)/shard_map/triangular_solve | solution.py:74
  942.5 46.1 %all-reduce.7.cloned.1.call-done = f32[256,1024]{1,0:T(8,128)} async-done(((f32[256,1024]{1,0:T(8,128)}), f32[256,1024]{1,0:T(8,128)}) %all-reduce.7.cloned.1.call-update) | async-done | bytes 1048592 | tf_op jit(solution)/shard_map/psum | solution.py:34
  988.6 49.1 %all-reduce.9.cloned.1.call-done = f32[256,1024]{1,0:T(8,128)} async-done(((f32[256,1024]{1,0:T(8,128)}), f32[256,1024]{1,0:T(8,128)}) %all-reduce.9.cloned.1.call-update) | async-done | bytes 1048592 | tf_op jit(solution)/shard_map/psum | solution.py:34
  1039.0 47.5 %all-reduce.11.cloned.1.call-done = f32[256,1024]{1,0:T(8,128)} async-done(((f32[256,1024]{1,0:T(8,128)}), f32[256,1024]{1,0:T(8,128)}) %all-reduce.11.cloned.1.call-update) | async-done | bytes 1048592 | tf_op jit(solution)/shard_map/psum | solution.py:34
  1086.7 17.0 %convolution_select_fusion = f32[2048,256]{1,0:T(8,128)} fusion(f32[2048,256]{1,0:T(8,128)S(1)} %bitcast.126, f32[2048,1024]{0,1:T(8,128)} %all-gather.2.cloned.1.call-done, f32[256,1024]{1,0:T(8,128)} %all-reduce.11.cloned.1.call-done, pred[2048]{0:T(1024)(128)(4,1)S(1)} %fusion.93), kind=kOutput, calls=%fused_computation.17 | convolution fusion | flops 6442975232 | bytes 13633536 | tf_op jit(solution)/shard_map/dot_general | solution.py:79
  (118 shorter events, 136.2 us)
Async XLA Ops:
  6.5 361.0 %all-reduce.13.cloned.1.call-start = ((), (), s32[]{:S(2)}) async-start(), calls=%async_computation.5 | async-start | bytes 12582912 | tf_op jit(solution)/shard_map/psum | solution.py:16
  24.3 3.0 copy-start.1
  396.8 11.3 %copy-start.3 = (bf16[4,256,1536]{2,1,0:T(8,128)(2,1)S(1)}, bf16[4,256,1536]{2,1,0:T(8,128)(2,1)}, u32[]{:S(2)}) copy-start(bf16[4,256,1536]{2,1,0:T(8,128)(2,1)} %get-tuple-element.22) | copy-start | bytes 9437188
  419.1 100.4 %all-to-all-start = ((f32[4,2048,256]{2,1,0:T(8,128)}), f32[4,2048,256]{2,1,0:T(8,128)}, u32[]{:S(2)}, u32[]{:S(2)}) async-start(f32[4,2048,256]{2,1,0:T(8,128)} %convolution_bitcast_fusion), calls=%async_computation | async-start | bytes 16777216 | tf_op jit(solution)/shard_map/all_to_all | solution.py:27
  424.8 167.6 %all-gather.2.cloned.1.call-start = ((), (), s32[]{:S(2)}) async-start(), calls=%async_computation.1 | async-start | bytes 10485760 | tf_op jit(solution)/shard_map/all_gather | solution.py:70
  531.2 457.4 %all-reduce.7.cloned.1.call-start = ((), (), s32[]{:S(2)}) async-start(), calls=%async_computation.2 | async-start | bytes 2097152 | tf_op jit(solution)/shard_map/psum | solution.py:34
  607.3 2.0 copy-start.2
  919.0 3.2 copy-start
  942.4 95.3 %all-reduce.9.cloned.1.call-start = ((), (), s32[]{:S(2)}) async-start(), calls=%async_computation.3 | async-start | bytes 2097152 | tf_op jit(solution)/shard_map/psum | solution.py:34
  988.6 97.9 %all-reduce.11.cloned.1.call-start = ((), (), s32[]{:S(2)}) async-start(), calls=%async_computation.4 | async-start | bytes 2097152 | tf_op jit(solution)/shard_map/psum | solution.py:34
Sparse Core Ops, SparseCore 0:
  30.6 336.8 all-reduce.12
  531.3 61.0 all-gather.1
  942.6 45.9 all-reduce.6
  990.9 46.7 all-reduce.8
  1039.9 46.5 all-reduce.10
where the time goes:
time: 1120 us; the launch traced here: 1110 us
  waiting for transfers between devices  604 us (54%)
  other arithmetic  276 us (25%)
  local copies, waits for them, and re-layouts  113 us (10%)
  matrix products  89.8 us (8%)
  between operations  21.5 us (2%)
    psum x1, waiting for transfers between devices, from_root(): return lax.psum(kept, axis)  310 us
    another operation x31, other arithmetic, local(): cholesky_factor = jnp.linalg.cholesky(diagonal)  173 us
    psum x3, waiting for transfers between devices, broadcast_by_axis(): value = lax.psum(value, axis)  143 us
    all_to_all x1, waiting for transfers between devices, summed_on_arrival(): lax.all_to_all(split_up(value, dim, devices), axis, 0, 0, tiled=True)  92.7 us
    another operation x3, other arithmetic, local(): lax.linalg.triangular_solve(cholesky_factor, identity, left_side=True, lo...  83.2 us
    all_gather x1, waiting for transfers between devices, local(): lax.all_gather(panel_tiles - own_sums, 'col', axis=1, tiled=True)  58.3 us
    another operation x14, matrix products, local(): cholesky_factor = jnp.linalg.cholesky(diagonal)  23.1 us
    another operation x24, local copies, waits for them, and re-layouts  23 us
  transfers between devices with their start and end apart: 6, of which 6 were waited for; matrix products, arithmetic and copies ran while one was open for 3% of the time, Pallas kernels for 0%

commit v1 on v0

--- a/solution.py
+++ b/solution.py
@@ -67,7 +67,9 @@
         preferred_element_type=jnp.float32,
     )
     own_sums = summed_on_arrival(update_terms, "col", 1)
-    updated_tiles = lax.all_gather(panel_tiles - own_sums, "col", axis=1, tiled=True)
+    part = panel_tiles - own_sums
+    outgoing = jnp.stack([part] * lax.axis_size("col"))
+    updated_tiles = jnp.concatenate(lax.all_to_all(outgoing, "col", 0, 0), axis=1)
     diagonal = lax.dynamic_slice_in_dim(updated_tiles, local_slot * TILE, TILE, 0)
     identity = jnp.eye(TILE, dtype=jnp.float32)
     cholesky_factor = jnp.linalg.cholesky(diagonal)

time: 1120 us -> 1160 us (1.036)
  blocking collectives: 0 us -> 98.6 us
  waiting for transfers between devices: 604 us -> 544 us
    all_to_all x0 -> x1, blocking collectives: none -> 98.6 us  [summed_on_arrival(): lax.all_to_all(split_up(value, dim, devices), axis, 0, 0, tiled=True)]
    all_gather x1 -> x0, waiting for transfers between devices: 58.3 us -> none  [local(): lax.all_gather(panel_tiles - own_sums, 'col', axis=1, tiled=True)]
    another operation x24 -> x25, local copies, waits for them, and re-layouts: 23 us -> 28.8 us
  transfers between devices with their start and end apart: 6 -> 5, of which waited for: 6 -> 5; matrix products, arithmetic and copies ran while one was open for 3% -> 3% of each run, Pallas kernels for 0% -> 0%
where the time goes in v1:
time: 1160 us; the launch traced here: 1150 us
  waiting for transfers between devices  544 us (47%)
  other arithmetic  276 us (24%)
  local copies, waits for them, and re-layouts  116 us (10%)
  blocking collectives  98.6 us (8%)
  matrix products  87.9 us (8%)
  between operations  21.5 us (2%)
    psum x1, waiting for transfers between devices, from_root(): return lax.psum(kept, axis)  310 us
    another operation x31, other arithmetic, local(): cholesky_factor = jnp.linalg.cholesky(diagonal)  173 us
    psum x3, waiting for transfers between devices, broadcast_by_axis(): value = lax.psum(value, axis)  142 us
    all_to_all x1, blocking collectives, summed_on_arrival(): lax.all_to_all(split_up(value, dim, devices), axis, 0, 0, tiled=True)  98.6 us
    all_to_all x1, waiting for transfers between devices, local(): lax.all_to_all(outgoing, 'col', 0, 0)  91.8 us
    another operation x3, other arithmetic, local(): lax.linalg.triangular_solve(cholesky_factor, identity, left_side=True, lo...  83.2 us
  transfers between devices with their start and end apart: 5, of which 5 were waited for; matrix products, arithmetic and copies ran while one was open for 3% of the time, Pallas kernels for 0%

profile of v1, /device:TPU:0, one launch (start us, length us, event | category | flops | bytes accessed | tf_op | source)
XLA Modules:
  0.0 1149.5 jit_solution(2286179789978974472)
XLA Ops:
  10.4 5.9 constant_dynamic-slice_fusion.3
  30.5 13.3 %reshape.140 = bf16[2,1024,6,256]{3,2,1,0:T(8,128)(2,1)} reshape(bf16[2048,1536]{1,0:T(8,128)(2,1)} %param.5) | data formatting | bytes 12582912 | tf_op jit(solution)/shard_map/reshape | solution.py:54
  43.8 13.4 %reshape.139 = bf16[2,1024,6,256]{3,2,1,0:T(8,128)(2,1)} reshape(bf16[2048,1536]{1,0:T(8,128)(2,1)} %param.6) | data formatting | bytes 12582912 | tf_op jit(solution)/shard_map/reshape | solution.py:55
  57.2 310.4 %all-reduce.13.cloned.1.call-done = (bf16[1024,6,256]{0,2,1:T(8,128)(2,1)}, bf16[4,256,1536]{2,1,0:T(8,128)(2,1)}) async-done(((bf16[1024,6,256]{0,2,1:T(8,128)(2,1)}, bf16[4,256,1536]{2,1,0:T(8,128)(2,1)}), (bf16[1024,6,256]{0,2,1:T(8,128)(2,1)}, bf16[4,256,1536]{2,1,0:T(8,128)(2,1)})) %all-reduce.13.cloned.1.call-update) | async-done | bytes 6291472 | tf_op jit(solution)/shard_map/psum | solution.py:16
  367.6 16.6 %convert_bitcast_fusion = bf16[2,1024,6,256]{1,3,2,0:T(8,128)(2,1)} fusion(bf16[2,1024,6,256]{3,2,1,0:T(8,128)(2,1)} %reshape.140, bf16[2,1024,6,256]{3,2,1,0:T(8,128)(2,1)} %reshape.139, bf16[1024,6,256]{0,2,1:T(8,128)(2,1)} %get-tuple-element.21), kind=kOutput, calls=%fused_computation.6 | convolution fusion | flops 3225157632 | bytes 22020096 | tf_op jit(solution)/shard_map/tbjr,tjrs->tbjs/dot_general | solution.py:60
  384.2 12.7 %copy.12 = bf16[2,1024,6,256]{1,0,3,2:T(2,128)(2,1)} copy(bf16[2,1024,6,256]{1,3,2,0:T(8,128)(2,1)} %convert_bitcast_fusion) | data formatting | bytes 12582912 | tf_op jit(solution)/shard_map/convert_element_type | solution.py:62
  396.8 11.3 reshape.143
  408.1 9.0 convolution_bitcast_fusion
  417.2 98.6 %all_to_all.10 = f32[4,2048,256]{2,1,0:T(8,128)} all-to-all(f32[4,2048,256]{2,1,0:T(8,128)S(1)} %convolution_bitcast_fusion), channel_id=1, replica_groups=mesh['row_0'=2,'row_1'=4,'row_2'=4,'col'=4] {'col'}, dimensions={0} | all-to-all | bytes 16777216 | tf_op jit(solution)/shard_map/all_to_all | solution.py:27
  525.6 5.9 stack.2
  540.0 91.8 %all-to-all-done.1 = f32[4,2048,256]{1,2,0:T(8,128)} async-done(((f32[4,2048,256]{1,2,0:T(8,128)}), f32[4,2048,256]{1,2,0:T(8,128)}, u32[]{:S(2)}, u32[]{:S(2)}) %all-to-all-start.1) | async-done | bytes 8388640 | tf_op jit(solution)/shard_map/all_to_all | solution.py:72
  648.8 11.7 %cholesky.223 = f32[128,128]{1,0:T(8,128)S(1)} custom-call(f32[128,128]{1,0:T(8,128)S(1)} %cholesky.580), custom_call_target="Cholesky" | custom-call | tf_op jit(solution)/shard_map/jit(cholesky)/cholesky | solution.py:75
  663.0 9.8 custom-call.62
  676.7 11.9 %cholesky.244 = f32[128,128]{1,0:T(8,128)S(1)} custom-call(f32[128,128]{1,0:T(8,128)S(1)} %cholesky.584), custom_call_target="Cholesky" | custom-call | tf_op jit(solution)/shard_map/jit(cholesky)/cholesky | solution.py:75
  689.2 9.8 custom-call.63
  702.4 11.7 %cholesky.468 = f32[128,128]{1,0:T(8,128)S(1)} custom-call(f32[128,128]{1,0:T(8,128)S(1)} %cholesky.589), custom_call_target="Cholesky" | custom-call | tf_op jit(solution)/shard_map/jit(cholesky)/cholesky | solution.py:75
  714.8 9.8 custom-call.64
  728.1 11.9 %cholesky.487 = f32[128,128]{1,0:T(8,128)S(1)} custom-call(f32[128,128]{1,0:T(8,128)S(1)} %cholesky.594), custom_call_target="Cholesky" | custom-call | tf_op jit(solution)/shard_map/jit(cholesky)/cholesky | solution.py:75
  740.7 9.8 custom-call.65
  754.0 11.7 %cholesky.506 = f32[128,128]{1,0:T(8,128)S(1)} custom-call(f32[128,128]{1,0:T(8,128)S(1)} %cholesky.599), custom_call_target="Cholesky" | custom-call | tf_op jit(solution)/shard_map/jit(cholesky)/cholesky | solution.py:75
  766.3 10.2 custom-call.66
  779.8 11.7 %cholesky.526 = f32[128,128]{1,0:T(8,128)S(1)} custom-call(f32[128,128]{1,0:T(8,128)S(1)} %cholesky.604), custom_call_target="Cholesky" | custom-call | tf_op jit(solution)/shard_map/jit(cholesky)/cholesky | solution.py:75
  792.2 9.8 custom-call.67
  805.0 11.7 %cholesky.546 = f32[128,128]{1,0:T(8,128)S(1)} custom-call(f32[128,128]{1,0:T(8,128)S(1)} %cholesky.609), custom_call_target="Cholesky" | custom-call | tf_op jit(solution)/shard_map/jit(cholesky)/cholesky | solution.py:75
  817.3 9.8 custom-call.68
  829.8 11.7 %cholesky.564 = f32[128,128]{1,0:T(8,128)S(1)} custom-call(f32[128,128]{1,0:T(8,128)S(1)} %convolution_subtract_fusion.11), custom_call_target="Cholesky" | custom-call | tf_op jit(solution)/shard_map/jit(cholesky)/cholesky | solution.py:75
  856.7 23.1 %while.1 = (s32[]{:T(128)}, f32[1024,1024]{1,0:T(8,128)}, s32[8,2]{0,1:T(2,128)S(1)}, f32[8,128,128]{2,1,0:T(8,128)S(1)}, s32[]{:T(128)}) while((s32[]{:T(128)}, f32[1024,1024]{1,0:T(8,128)}, s32[8,2]{0,1:T(2,128)S(1)}, f32[8,128,128]{2,1,0:T(8,128)S(1)}, s32[]{:T(128)}) %tuple.58), condition=%wide.while_cond, body=%wide.while_body.sunk | while | flops 2 | bytes 131189 | solution.py:76
  879.8 78.8 %custom-call.69 = f32[8,128,128]{1,2,0:T(8,128)S(1)} custom-call(f32[8,128,128]{2,1,0:T(8,128)S(1)} %get-tuple-element.12), custom_call_target="InvertDiagBlocksLowerTriangular" | custom-call | tf_op jit(solution)/shard_map/triangular_solve | solution.py:76
  982.1 45.3 %all-reduce.7.cloned.1.call-done = f32[256,1024]{1,0:T(8,128)} async-done(((f32[256,1024]{1,0:T(8,128)}), f32[256,1024]{1,0:T(8,128)}) %all-reduce.7.cloned.1.call-update) | async-done | bytes 1048592 | tf_op jit(solution)/shard_map/psum | solution.py:34
  1027.4 49.2 %all-reduce.9.cloned.1.call-done = f32[256,1024]{1,0:T(8,128)} async-done(((f32[256,1024]{1,0:T(8,128)}), f32[256,1024]{1,0:T(8,128)}) %all-reduce.9.cloned.1.call-update) | async-done | bytes 1048592 | tf_op jit(solution)/shard_map/psum | solution.py:34
  1077.9 47.5 %all-reduce.11.cloned.1.call-done = f32[256,1024]{1,0:T(8,128)} async-done(((f32[256,1024]{1,0:T(8,128)}), f32[256,1024]{1,0:T(8,128)}) %all-reduce.11.cloned.1.call-update) | async-done | bytes 1048592 | tf_op jit(solution)/shard_map/psum | solution.py:34
  1125.6 17.0 %convolution_select_fusion = f32[2048,256]{1,0:T(8,128)} fusion(f32[2048,256]{1,0:T(8,128)S(1)} %bitcast.129, f32[2048,1024]{0,1:T(8,128)} %bitcast.7, f32[256,1024]{1,0:T(8,128)} %all-reduce.11.cloned.1.call-done, pred[2048]{0:T(1024)(128)(4,1)S(1)} %fusion.93), kind=kOutput, calls=%fused_computation.17 | convolution fusion | flops 6442975232 | bytes 13633536 | tf_op jit(solution)/shard_map/dot_general | solution.py:81
  (116 shorter events, 138.2 us)
Async XLA Ops:
  6.5 361.0 %all-reduce.13.cloned.1.call-start = ((), (), s32[]{:S(2)}) async-start(), calls=%async_computation.5 | async-start | bytes 12582912 | tf_op jit(solution)/shard_map/psum | solution.py:16
  24.3 3.0 copy-start.1
  396.8 11.3 copy-start.3
  531.5 100.3 %all-to-all-start.1 = ((f32[4,2048,256]{1,2,0:T(8,128)}), f32[4,2048,256]{1,2,0:T(8,128)}, u32[]{:S(2)}, u32[]{:S(2)}) async-start(f32[4,2048,256]{1,2,0:T(8,128)} %stack.2), calls=%async_computation.1 | async-start | bytes 16777216 | tf_op jit(solution)/shard_map/all_to_all | solution.py:72
  537.1 490.2 %all-reduce.7.cloned.1.call-start = ((), (), s32[]{:S(2)}) async-start(), calls=%async_computation.2 | async-start | bytes 2097152 | tf_op jit(solution)/shard_map/psum | solution.py:34
  646.8 2.0 copy-start.2
  958.6 3.2 copy-start
  982.0 94.6 %all-reduce.9.cloned.1.call-start = ((), (), s32[]{:S(2)}) async-start(), calls=%async_computation.3 | async-start | bytes 2097152 | tf_op jit(solution)/shard_map/psum | solution.py:34
  1027.3 98.1 %all-reduce.11.cloned.1.call-start = ((), (), s32[]{:S(2)}) async-start(), calls=%async_computation.4 | async-start | bytes 2097152 | tf_op jit(solution)/shard_map/psum | solution.py:34
Sparse Core Ops, SparseCore 0:
  30.6 336.8 all-reduce.12
  982.1 45.1 all-reduce.6
  1029.8 46.7 all-reduce.8
  1078.8 46.5 all-reduce.10
